TPU v7x, 32 devices: a whole 2x2x4 slice. The times are simulated.
32 devices in a mesh: expert: 8 (over z, x), dp: 4 (over y, core).
Axes of the slice: x: 2, y: 2, z: 4, core: 2. Of those that a mesh axis runs over, the one named last changes fastest.
Arguments:
- tokens: bfloat16 [4096, 2048], P(('expert', 'dp')), may hold values from -6 to 6
- expert_index: int32 [4096, 4], P(('expert', 'dp')), may hold values from 0 to 7, all different within a row; in each aligned block of 128 rows (0 to 127, 128 to 255, ...) at most 96 rows name the same one
- gate_weights: bfloat16 [4096, 4], P(('expert', 'dp')), may hold values from 0.19921875 to 1
- w_gate: bfloat16 [8, 2048, 768], P('expert'), may hold values from -0.125 to 0.125
- w_up: bfloat16 [8, 2048, 768], P('expert'), may hold values from -0.125 to 0.125
- w_down: bfloat16 [8, 768, 2048], P('expert'), may hold values from -0.21875 to 0.21875
- v_gate: bfloat16 [8, 2048, 768], P('expert'), may hold values from -0.125 to 0.125
- v_up: bfloat16 [8, 2048, 768], P('expert'), may hold values from -0.125 to 0.125
- curvature: bfloat16 [2048, 2048], replicated, may hold values from -0.4 to 3.4, as said below
Outputs:
- hvp_gate: float32 [8, 768, 2048], P('expert', 'dp')
- hvp_up: float32 [8, 768, 2048], P('expert', 'dp')
- input_tangent: bfloat16 [4096, 2048], P(('expert', 'dp'))
Inputs may be any that keep to these rules, and one draw needn't show every extreme that they name: `expert_index`: the 4 experts of a token differ. Among the rows of one device no expert is named more than 96 times, and in some device's rows one expert is named exactly 96 times. `curvature`: Symmetric.
All inputs are finite; a program needn't handle non-finite values.
Results may differ from a plain program's by a relative error of at most 0.014.
Values may be sent and summed in bfloat16 or wider, within the bound.
A program may use at most 128 MiB of HBM per device.

v0:
```python
import jax
import jax.numpy as jnp
from jax import lax
from jax.sharding import PartitionSpec as P

EXP_DEV = 1


def slot_numbers(route_ids, expert_total):
    flat_ids = route_ids.reshape(-1)
    onehot = (flat_ids[:, None] == jnp.arange(expert_total, dtype=jnp.int32)[None, :]).astype(
        jnp.int32
    )
    before = jnp.cumsum(onehot, axis=0) * onehot
    return (jnp.sum(before, axis=1) - 1).reshape(route_ids.shape)


def shards(tokens, expert_index, gate_weights, w_gate, w_up, w_down, v_gate, v_up, curvature):
    expert_total = lax.axis_size("expert") * EXP_DEV
    tok_count, model_width = tokens.shape
    top_count = expert_index.shape[1]
    capacity = 3 * tok_count * top_count // (2 * expert_total)
    slot_total = expert_total * capacity
    slot_own = expert_index * capacity + slot_numbers(expert_index, expert_total)
    slot_match = slot_own[None, :, :] == jnp.arange(slot_total, dtype=jnp.int32)[:, None, None]
    pick_table = jnp.any(slot_match, axis=2).astype(jnp.bfloat16)
    slot_gates = jnp.sum(
        jnp.where(slot_match, gate_weights.astype(jnp.float32)[None, :, :], 0.0), axis=(1, 2)
    ).astype(jnp.bfloat16)
    sent_rows = jnp.dot(pick_table, tokens, preferred_element_type=jnp.float32).astype(jnp.bfloat16)
    recv_rows, recv_gates = (
        lax.all_to_all(
            sent_rows.reshape(expert_total, capacity, model_width),
            "expert",
            split_axis=0,
            concat_axis=0,
            tiled=True,
        ),
        lax.all_to_all(
            slot_gates.reshape(expert_total, capacity),
            "expert",
            split_axis=0,
            concat_axis=0,
            tiled=True,
        ),
    )
    in_rows = recv_rows.reshape(-1, model_width)
    row_gates = recv_gates.reshape(-1, 1).astype(jnp.float32)
    gate_pre = jnp.dot(in_rows, w_gate[0], preferred_element_type=jnp.float32)
    up_pre = jnp.dot(in_rows, w_up[0], preferred_element_type=jnp.float32)
    gate_tan = jnp.dot(in_rows, v_gate[0], preferred_element_type=jnp.float32)
    up_tan = jnp.dot(in_rows, v_up[0], preferred_element_type=jnp.float32)
    sigmoid_val = jax.nn.sigmoid(gate_pre)
    silu_val = gate_pre * sigmoid_val
    silu_slope = sigmoid_val * (1.0 + gate_pre * (1.0 - sigmoid_val))
    hidden_tan = (silu_slope * up_pre * gate_tan + silu_val * up_tan).astype(jnp.bfloat16)
    routed_out = (
        row_gates * jnp.dot(hidden_tan, w_down[0], preferred_element_type=jnp.float32)
    ).astype(jnp.bfloat16)
    came_back = lax.all_to_all(
        routed_out.reshape(expert_total, capacity, model_width),
        "expert",
        split_axis=0,
        concat_axis=0,
        tiled=True,
    )
    token_tan = lax.dot_general(
        pick_table,
        came_back.reshape(-1, model_width),
        (((0,), (0,)), ((), ())),
        preferred_element_type=jnp.float32,
    ).astype(jnp.bfloat16)
    curved = jnp.dot(token_tan, curvature, preferred_element_type=jnp.float32).astype(jnp.bfloat16)
    sent_curved = jnp.dot(pick_table, curved, preferred_element_type=jnp.float32).astype(
        jnp.bfloat16
    )
    recv_curved = lax.all_to_all(
        sent_curved.reshape(expert_total, capacity, model_width),
        "expert",
        split_axis=0,
        concat_axis=0,
        tiled=True,
    ).reshape(-1, model_width)
    back_hidden = row_gates * lax.dot_general(
        recv_curved, w_down[0], (((1,), (1,)), ((), ())), preferred_element_type=jnp.float32
    )
    gate_bar = (back_hidden * up_pre * silu_slope).astype(jnp.bfloat16)
    up_bar = (back_hidden * silu_val).astype(jnp.bfloat16)
    gate_term = lax.dot_general(
        gate_bar, in_rows, (((0,), (0,)), ((), ())), preferred_element_type=jnp.float32
    )
    up_term = lax.dot_general(
        up_bar, in_rows, (((0,), (0,)), ((), ())), preferred_element_type=jnp.float32
    )
    hvp_gate = lax.psum_scatter(
        gate_term[None].astype(jnp.bfloat16), "dp", scatter_dimension=1, tiled=True
    ).astype(jnp.float32)
    hvp_up = lax.psum_scatter(
        up_term[None].astype(jnp.bfloat16), "dp", scatter_dimension=1, tiled=True
    ).astype(jnp.float32)
    route_in = lax.dot_general(
        gate_bar, w_gate[0], (((1,), (1,)), ((), ())), preferred_element_type=jnp.float32
    )
    route_in = route_in + lax.dot_general(
        up_bar, w_up[0], (((1,), (1,)), ((), ())), preferred_element_type=jnp.float32
    )
    route_in = route_in.astype(jnp.bfloat16)
    came_in = lax.all_to_all(
        route_in.reshape(expert_total, capacity, model_width),
        "expert",
        split_axis=0,
        concat_axis=0,
        tiled=True,
    )
    input_tangent = lax.dot_general(
        pick_table,
        came_in.reshape(-1, model_width),
        (((0,), (0,)), ((), ())),
        preferred_element_type=jnp.float32,
    ).astype(jnp.bfloat16)
    return (hvp_gate, hvp_up, input_tangent)


def solution(mesh):
    return jax.shard_map(
        shards,
        mesh=mesh,
        in_specs=(
            P(("expert", "dp"), None),
            P(("expert", "dp"), None),
            P(("expert", "dp"), None),
            P("expert", None, None),
            P("expert", None, None),
            P("expert", None, None),
            P("expert", None, None),
            P("expert", None, None),
            P(),
        ),
        out_specs=(P("expert", "dp", None), P("expert", "dp", None), P(("expert", "dp"), None)),
        check_vma=False,
    )
```

profile of v0, /device:TPU:0, one launch (start us, length us, event | category | flops | bytes accessed | tf_op | source)
XLA Modules:
  0.0 407.2 jit_solution(8314031828430436538)
XLA Ops:
  7.2 0.9 copy.31
  8.3 0.7 convert_element_type.83
  9.0 1.1 reduce-window.6
  10.2 0.2 slice_reduce_fusion
  10.7 0.7 multiply_add_fusion
  11.4 0.2 select_reduce_fusion
  11.6 0.7 convert_element_type.105
  12.3 7.3 %all-to-all-start = ((bf16[8,1,96]{2,1,0:T(2,128)(2,1)}), bf16[8,1,96]{2,1,0:T(2,128)(2,1)S(1)}, u32[]{:S(2)}, u32[]{:S(2)}) async-start(bf16[8,1,96]{2,1,0:T(2,128)(2,1)} %convert_element_type.105), calls=%async_computation | async-start | bytes 8192 | tf_op jit(solution)/shard_map/all_to_all | solution.py:39
  19.6 0.2 fusion.19
  19.8 3.7 convolution_convert_fusion.3
  23.5 2.5 all-to-all-done
  26.0 4.4 %all-to-all-start.1 = ((bf16[8,96,2048]{2,1,0:T(8,128)(2,1)}), bf16[8,96,2048]{2,1,0:T(8,128)(2,1)}, u32[]{:S(2)}, u32[]{:S(2)}) async-start(bf16[8,96,2048]{2,1,0:T(8,128)(2,1)} %bitcast.66), calls=%async_computation.1 | async-start | bytes 6291456 | tf_op jit(solution)/shard_map/all_to_all | solution.py:32
  30.4 0.2 reduce-scatter.5.cloned.1.call-start
  30.7 69.2 %all-to-all-done.1 = bf16[8,96,2048]{2,1,0:T(8,128)(2,1)} async-done(((bf16[8,96,2048]{2,1,0:T(8,128)(2,1)}), bf16[8,96,2048]{2,1,0:T(8,128)(2,1)}, u32[]{:S(2)}, u32[]{:S(2)}) %all-to-all-start.1) | async-done | bytes 3145760 | tf_op jit(solution)/shard_map/all_to_all | solution.py:32
  100.0 7.1 %fusion.8 = f32[768,768]{1,0:T(8,128)} fusion(bf16[768,2048]{1,0:T(8,128)(2,1)} %bitcast.3, bf16[1,2048,768]{2,1,0:T(8,128)(2,1)} %param.13), kind=kOutput, calls=%fused_computation.14 | convolution fusion | flops 2415919104 | bytes 8650752 | tf_op jit(solution)/shard_map/dot_general | solution.py:50
  107.0 6.1 %fusion.12 = f32[768,768]{1,0:T(8,128)} fusion(bf16[768,2048]{1,0:T(8,128)(2,1)} %bitcast.3, bf16[1,2048,768]{2,1,0:T(8,128)(2,1)S(1)} %copy-done.3), kind=kOutput, calls=%fused_computation.18 | convolution fusion | flops 2415919104 | bytes 8650752 | tf_op jit(solution)/shard_map/dot_general | solution.py:49
  113.1 6.0 %fusion.3 = f32[768,768]{1,0:T(8,128)} fusion(bf16[768,2048]{1,0:T(8,128)(2,1)} %bitcast.3, bf16[1,2048,768]{2,1,0:T(8,128)(2,1)S(1)} %copy-done.2), kind=kOutput, calls=%fused_computation.9 | convolution fusion | flops 2415919104 | bytes 8650752 | tf_op jit(solution)/shard_map/dot_general | solution.py:52
  119.1 12.6 %multiply_convert_fusion = bf16[768,2048]{1,0:T(8,128)(2,1)} fusion(bf16[1,768,2048]{2,1,0:T(8,128)(2,1)S(1)} %copy-done, f32[768]{0:T(1024)S(1)} %reshape.90, f32[768,768]{1,0:T(8,128)} %fusion.3, f32[768,768]{1,0:T(8,128)} %fusion.8, bf16[768,2048]{1,0:T(8,128)(2,1)} %bitcast.3, bf16[1,2048,768]{2,1,0:T(8,128)(2,1)} %param.15, f32[768,768]{1,0:T(8,128)} %fusion.12), kind=kOutput, calls=%fused_computation.1 | convolution fusion | flops 4842651648 | bytes 19663872 | tf_op jit(solution)/shard_map/dot_general | solution.py:58
  131.7 74.5 %all_to_all.26 = bf16[8,96,2048]{2,1,0:T(8,128)(2,1)S(1)} all-to-all(bf16[8,96,2048]{2,1,0:T(8,128)(2,1)} %bitcast.71), channel_id=1, replica_groups=mesh['expert'=8,'dp'=4] {'expert'}, dimensions={0} | all-to-all | bytes 6291456 | tf_op jit(solution)/shard_map/all_to_all | solution.py:60
  206.2 1.4 convolution_convert_fusion.6
  207.6 7.3 %convolution_convert_fusion.2 = bf16[768,2048]{1,0:T(8,128)(2,1)} fusion(pred[768,128]{1,0:T(8,128)(4,1)S(1)} %fusion.19, bf16[128,2048]{1,0:T(8,128)(2,1)} %convolution_convert_fusion.6, bf16[2048,2048]{1,0:T(8,128)(2,1)} %param.17), kind=kOutput, calls=%fused_computation.4 | convolution fusion | flops 1478230016 | bytes 12156928 | tf_op jit(solution)/shard_map/dot_general | solution.py:74
  215.0 74.4 %all_to_all.27 = bf16[8,96,2048]{2,1,0:T(8,128)(2,1)S(1)} all-to-all(bf16[8,96,2048]{2,1,0:T(8,128)(2,1)} %bitcast.65), channel_id=1, replica_groups=mesh['expert'=8,'dp'=4] {'expert'}, dimensions={0} | all-to-all | bytes 6291456 | tf_op jit(solution)/shard_map/all_to_all | solution.py:77
  289.4 4.3 %multiply_convert_fusion.1 = (bf16[768,768]{1,0:T(8,128)(2,1)S(1)}, bf16[768,768]{1,0:T(8,128)(2,1)}) fusion(f32[768]{0:T(1024)S(1)} %reshape.90, f32[768,768]{1,0:T(8,128)S(1)} %copy-done.6, f32[768,768]{1,0:T(8,128)S(1)} %copy-done.5, bf16[768,2048]{1,0:T(8,128)(2,1)S(1)} %bitcast.69, bf16[1,768,2048]{2,1,0:T(8,128)(2,1)S(1)} %copy-done), kind=kOutput, calls=%fused_computation.25 | convolution fusion | flops 2424176640 | bytes 13372416 | tf_op jit(solution)/shard_map/dot_general | solution.py:84
  293.7 1.0 copy-done.7
  294.7 5.9 %fusion.15 = bf16[1,768,2048]{2,1,0:T(8,128)(2,1)} fusion(bf16[768,768]{1,0:T(8,128)(2,1)S(1)} %get-tuple-element.3, bf16[768,2048]{1,0:T(8,128)(2,1)} %bitcast.3), kind=kOutput, calls=%fused_computation.21 | convolution fusion | flops 2417491968 | bytes 7471104 | tf_op jit(solution)/shard_map/dot_general | solution.py:92
  300.7 6.7 %fusion.14 = bf16[1,768,2048]{2,1,0:T(8,128)(2,1)} fusion(bf16[768,768]{1,0:T(8,128)(2,1)} %get-tuple-element.4, bf16[768,2048]{1,0:T(8,128)(2,1)} %bitcast.3), kind=kOutput, calls=%fused_computation.20 | convolution fusion | flops 2417491968 | bytes 7471104 | tf_op jit(solution)/shard_map/dot_general | solution.py:89
  307.5 6.0 %fusion.10 = f32[768,2048]{1,0:T(8,128)} fusion(bf16[768,768]{1,0:T(8,128)(2,1)} %get-tuple-element.4, bf16[1,2048,768]{2,1,0:T(8,128)(2,1)S(1)} %copy-done.4), kind=kOutput, calls=%fused_computation.16 | convolution fusion | flops 2415919104 | bytes 10616832 | tf_op jit(solution)/shard_map/dot_general | solution.py:101
  313.5 6.8 %add_convert_fusion = bf16[768,2048]{1,0:T(8,128)(2,1)S(1)} fusion(f32[768,2048]{1,0:T(8,128)} %fusion.10, bf16[768,768]{1,0:T(8,128)(2,1)} %copy-done.7, bf16[1,2048,768]{2,1,0:T(8,128)(2,1)} %param.13), kind=kOutput, calls=%fused_computation | convolution fusion | flops 2419064832 | bytes 13762560 | tf_op jit(solution)/shard_map/dot_general | solution.py:104
  320.3 73.7 %all_to_all.28 = bf16[8,96,2048]{2,1,0:T(8,128)(2,1)S(1)} all-to-all(bf16[8,96,2048]{2,1,0:T(8,128)(2,1)S(1)} %bitcast.70), channel_id=1, replica_groups=mesh['expert'=8,'dp'=4] {'expert'}, dimensions={0} | all-to-all | bytes 6291456 | tf_op jit(solution)/shard_map/all_to_all | solution.py:108
  394.0 1.4 convolution_convert_fusion.5
  395.4 2.5 convert_element_type.101
  397.9 2.5 convert_element_type.97
  (31 shorter events, 0.7 us)
Async XLA Ops:
  7.2 112.0 %copy-start = (bf16[1,768,2048]{2,1,0:T(8,128)(2,1)S(1)}, bf16[1,768,2048]{2,1,0:T(8,128)(2,1)}, u32[]{:S(2)}) copy-start(bf16[1,768,2048]{2,1,0:T(8,128)(2,1)} %param.14) | copy-start | bytes 9437188
  12.3 13.6 %all-to-all-start = ((bf16[8,1,96]{2,1,0:T(2,128)(2,1)}), bf16[8,1,96]{2,1,0:T(2,128)(2,1)S(1)}, u32[]{:S(2)}, u32[]{:S(2)}) async-start(bf16[8,1,96]{2,1,0:T(2,128)(2,1)} %convert_element_type.105), calls=%async_computation | async-start | bytes 8192 | tf_op jit(solution)/shard_map/all_to_all | solution.py:39
  26.0 74.0 %all-to-all-start.1 = ((bf16[8,96,2048]{2,1,0:T(8,128)(2,1)}), bf16[8,96,2048]{2,1,0:T(8,128)(2,1)}, u32[]{:S(2)}, u32[]{:S(2)}) async-start(bf16[8,96,2048]{2,1,0:T(8,128)(2,1)} %bitcast.66), calls=%async_computation.1 | async-start | bytes 6291456 | tf_op jit(solution)/shard_map/all_to_all | solution.py:32
  30.4 365.0 %reduce-scatter.5.cloned.1.call-start = ((), (), s32[]{:S(2)}) async-start(), calls=%async_computation.8 | async-start | bytes 3932160 | tf_op jit(solution)/shard_map/reduce_scatter | solution.py:98
  100.0 7.1 %copy-start.3 = (bf16[1,2048,768]{2,1,0:T(8,128)(2,1)S(1)}, bf16[1,2048,768]{2,1,0:T(8,128)(2,1)}, u32[]{:S(2)}) copy-start(bf16[1,2048,768]{2,1,0:T(8,128)(2,1)} %param.12) | copy-start | bytes 9437188
  107.0 6.1 %copy-start.2 = (bf16[1,2048,768]{2,1,0:T(8,128)(2,1)S(1)}, bf16[1,2048,768]{2,1,0:T(8,128)(2,1)}, u32[]{:S(2)}) copy-start(bf16[1,2048,768]{2,1,0:T(8,128)(2,1)} %param.16) | copy-start | bytes 9437188
  215.0 74.4 %copy-start.5 = (f32[768,768]{1,0:T(8,128)S(1)}, f32[768,768]{1,0:T(8,128)}, u32[]{:S(2)}) copy-start(f32[768,768]{1,0:T(8,128)} %fusion.8) | copy-start | bytes 7077892
  215.0 74.4 %copy-start.6 = (f32[768,768]{1,0:T(8,128)S(1)}, f32[768,768]{1,0:T(8,128)}, u32[]{:S(2)}) copy-start(f32[768,768]{1,0:T(8,128)} %fusion.12) | copy-start | bytes 7077892
  293.7 1.0 copy-start.7
  300.7 97.2 %reduce-scatter.3.cloned.1.call-start = ((), (), s32[]{:S(2)}) async-start(), calls=%async_computation.7 | async-start | bytes 3932160 | tf_op jit(solution)/shard_map/reduce_scatter | solution.py:95
  300.7 6.8 %copy-start.4 = (bf16[1,2048,768]{2,1,0:T(8,128)(2,1)S(1)}, bf16[1,2048,768]{2,1,0:T(8,128)(2,1)}, u32[]{:S(2)}) copy-start(bf16[1,2048,768]{2,1,0:T(8,128)(2,1)} %param.12) | copy-start | bytes 9437188
  394.0 6.3 %copy-start.1 = (bf16[1,768,2048]{2,1,0:T(8,128)(2,1)S(1)}, bf16[1,768,2048]{2,1,0:T(8,128)(2,1)}, u32[]{:S(2)}) copy-start(bf16[1,768,2048]{2,1,0:T(8,128)(2,1)} %param.14) | copy-start | bytes 9437188
Sparse Core Ops, SparseCore 0:
  300.8 36.8 reduce-scatter.4
  340.4 37.9 reduce-scatter.2
where the time goes:
time: 408 us; the launch traced here: 407 us
  blocking collectives  223 us (55%)
  matrix products  75.5 us (19%)
  waiting for transfers between devices  71.7 us (18%)
  between operations  14.1 us (3%)
  starting transfers between devices  12 us (3%)
  other arithmetic  8.04 us (2%)
    all_to_all x1, blocking collectives, shards(): lax.all_to_all(routed_out.reshape(expert_total, capacity, model_width), '...  74.5 us
    all_to_all x1, blocking collectives, shards(): lax.all_to_all(sent_curved.reshape(expert_total, capacity, model_width),...  74.4 us
    all_to_all x1, blocking collectives, shards(): lax.all_to_all(route_in.reshape(expert_total, capacity, model_width), 'ex...  73.7 us
    all_to_all x1, waiting for transfers between devices, shards(): lax.all_to_all(sent_rows.reshape(expert_total, capacity, model_width), 'e...  69.2 us
    dot_general x1, matrix products, shards(): jnp.dot(hidden_tan, w_down[0], preferred_element_type=jnp.float32)  12.6 us
  transfers between devices with their start and end apart: 4, of which 2 were waited for; matrix products, arithmetic and copies ran while one was open for 7% of the time, Pallas kernels for 0%

commit v1 on v0

v1 whole, which is shorter than its diff:
```python
import functools

import jax
import jax.numpy as jnp
from jax import lax
from jax.experimental import pallas as pl
from jax.experimental.pallas import tpu as pltpu
from jax.sharding import PartitionSpec as P

BF = jnp.bfloat16
F32 = jnp.float32
MESH = pl.DeviceIdType.MESH


def dot(a, b, ca=1, cb=0):
    return lax.dot_general(a, b, (((ca,), (cb,)), ((), ())), preferred_element_type=F32)


def peers(nz, nx):
    me = lax.axis_index("expert")
    return me, lax.div(me, nx), lax.rem(me, nx)


def greet(nz, nx):
    me, z, x = peers(nz, nx)
    barrier = pltpu.get_barrier_semaphore()

    def hello(target):
        pl.semaphore_signal(barrier, inc=1, device_id={"expert": target}, device_id_type=MESH)

    for k in range(1, nx):
        hello(z * nx + lax.rem(x + k, nx))

    @pl.when(z < nz - 1)
    def _():
        hello(me + nx)

    @pl.when(z > 0)
    def _():
        hello(me - nx)

    ends = (z == 0).astype(jnp.int32) + (z == nz - 1).astype(jnp.int32)
    pl.semaphore_wait(barrier, nx + 1 - ends)


def remote(src, dst, send_sem, recv_sem, target):
    return pltpu.make_async_remote_copy(
        src_ref=src,
        dst_ref=dst,
        send_sem=send_sem,
        recv_sem=recv_sem,
        device_id={"expert": target},
        device_id_type=MESH,
    )


def gather_kernel(nz, nx, count, *refs):
    ins, outs = refs[:count], refs[count : 2 * count]
    own_sem, up_sem, down_sem, side_sem, recv_sem = refs[2 * count :]
    me, z, x = peers(nz, nx)
    greet(nz, nx)

    def up(i, src, zs):
        slot = zs * nx + x
        return remote(src, outs[i].at[slot], up_sem.at[i, zs], recv_sem.at[i, slot], me + nx)

    def down(i, src, zs):
        slot = zs * nx + x
        return remote(src, outs[i].at[slot], down_sem.at[i, zs], recv_sem.at[i, slot], me - nx)

    def side(i, src, zs, k):
        slot = zs * nx + x
        target = z * nx + lax.rem(x + k, nx)
        return remote(src, outs[i].at[slot], side_sem.at[i, zs, k], recv_sem.at[i, slot], target)

    def arrived(i, slot):
        here = outs[i].at[slot]
        remote(here, here, own_sem.at[i], recv_sem.at[i, slot], z * nx + lax.rem(x + 1, nx)).wait_recv()

    def copy_own(i):
        return pltpu.make_async_copy(ins[i], outs[i].at[me], own_sem.at[i])

    for i in range(count):
        for k in range(1, nx):
            side(i, ins[i], z, k).start()

        @pl.when(z < nz - 1)
        def _():
            up(i, ins[i], z).start()

        @pl.when(z > 0)
        def _():
            down(i, ins[i], z).start()

        copy_own(i).start()
    for d in range(1, nz):
        for i in range(count):

            @pl.when(z - d >= 0)
            def _():
                slot = (z - d) * nx + x
                arrived(i, slot)

                @pl.when(z < nz - 1)
                def _():
                    up(i, outs[i].at[slot], z - d).start()

                for k in range(1, nx):
                    side(i, outs[i].at[slot], z - d, k).start()

            @pl.when(z + d < nz)
            def _():
                slot = (z + d) * nx + x
                arrived(i, slot)

                @pl.when(z > 0)
                def _():
                    down(i, outs[i].at[slot], z + d).start()

                for k in range(1, nx):
                    side(i, outs[i].at[slot], z + d, k).start()

    for i in range(count):
        for zs in range(nz):
            slot = zs * nx + x
            for k in range(1, nx):
                arrived(i, zs * nx + lax.rem(x + k, nx))
                side(i, ins[i], zs, k).wait_send()

            @pl.when((z < nz - 1) & (zs <= z))
            def _():
                up(i, ins[i], zs).wait_send()

            @pl.when((z > 0) & (zs >= z))
            def _():
                down(i, ins[i], zs).wait_send()

        copy_own(i).wait()


def scatter_kernel(nz, nx, p_ref, out_ref, side_buf, up_buf, down_buf, stage, acc, side_send, side_recv, line_send, line_recv):
    me, z, x = peers(nz, nx)
    greet(nz, nx)

    def side(zd, k):
        peer = lax.rem(x + k, nx)
        return remote(
            p_ref.at[zd * nx + peer], side_buf.at[zd, k - 1], side_send.at[zd, k - 1],
            side_recv.at[zd, k - 1], z * nx + peer,
        )

    def up(zd):
        return remote(stage.at[zd], up_buf.at[zd], line_send.at[0, zd], line_recv.at[0, zd], me + nx)

    def down(zd):
        return remote(stage.at[zd], down_buf.at[zd], line_send.at[1, zd], line_recv.at[1, zd], me - nx)

    def begin(zd):
        for k in range(1, nx):
            side(zd, k).start()

    def total(zd):
        for k in range(1, nx):
            side(zd, k).wait_recv()
        value = p_ref[zd * nx + x].astype(F32)
        for k in range(1, nx):
            value = value + side_buf[zd, k - 1].astype(F32)
        acc[...] = value

    def from_below(zd):
        @pl.when(z > 0)
        def _():
            up(zd).wait_recv()
            acc[...] += up_buf[zd].astype(F32)

    def from_above(zd):
        @pl.when(z < nz - 1)
        def _():
            down(zd).wait_recv()
            acc[...] += down_buf[zd].astype(F32)

    for d in range(nz - 1, 0, -1):

        @pl.when(z + d < nz)
        def _():
            begin(z + d)

        @pl.when(z - d >= 0)
        def _():
            begin(z - d)

    begin(z)
    for d in range(nz - 1, 0, -1):

        @pl.when(z + d < nz)
        def _():
            total(z + d)
            from_below(z + d)
            stage[z + d] = acc[...].astype(BF)
            up(z + d).start()

        @pl.when(z - d >= 0)
        def _():
            total(z - d)
            from_above(z - d)
            stage[z - d] = acc[...].astype(BF)
            down(z - d).start()

    total(z)
    from_below(z)
    from_above(z)
    out_ref[...] = acc[...].astype(BF)
    for zd in range(nz):
        for k in range(1, nx):
            side(zd, k).wait_send()

        @pl.when(zd > z)
        def _():
            up(zd).wait_send()

        @pl.when(zd < z)
        def _():
            down(zd).wait_send()


def gather(nz, nx, number, *arrays):
    n, m = nz * nx, len(arrays)
    made = pl.pallas_call(
        functools.partial(gather_kernel, nz, nx, m),
        out_shape=[jax.ShapeDtypeStruct((n, *a.shape), a.dtype) for a in arrays],
        in_specs=[pl.BlockSpec(memory_space=pl.ANY)] * m,
        out_specs=[pl.BlockSpec(memory_space=pl.ANY)] * m,
        scratch_shapes=[
            pltpu.SemaphoreType.DMA((m,)),
            pltpu.SemaphoreType.DMA((m, nz)),
            pltpu.SemaphoreType.DMA((m, nz)),
            pltpu.SemaphoreType.DMA((m, nz, nx)),
            pltpu.SemaphoreType.DMA((m, n)),
        ],
        compiler_params=pltpu.CompilerParams(collective_id=number, has_side_effects=True),
    )(*arrays)
    return [a.reshape(-1, a.shape[-1]) for a in made]


def scatter(nz, nx, number, p):
    rows, width = p.shape[0] // (nz * nx), p.shape[1]
    block = (rows, width)
    return pl.pallas_call(
        functools.partial(scatter_kernel, nz, nx),
        out_shape=jax.ShapeDtypeStruct(block, BF),
        in_specs=[pl.BlockSpec(memory_space=pltpu.VMEM)],
        out_specs=pl.BlockSpec(memory_space=pltpu.VMEM),
        scratch_shapes=[
            pltpu.VMEM((nz, max(nx - 1, 1), *block), BF),
            pltpu.VMEM((nz, *block), BF),
            pltpu.VMEM((nz, *block), BF),
            pltpu.VMEM((nz, *block), BF),
            pltpu.VMEM(block, F32),
            pltpu.SemaphoreType.DMA((nz, max(nx - 1, 1))),
            pltpu.SemaphoreType.DMA((nz, max(nx - 1, 1))),
            pltpu.SemaphoreType.DMA((2, nz)),
            pltpu.SemaphoreType.DMA((2, nz)),
        ],
        compiler_params=pltpu.CompilerParams(
            collective_id=number, has_side_effects=True, vmem_limit_bytes=48 * 2**20
        ),
    )(p.reshape(nz * nx, *block))


def shards(
    nz, nx, tokens, expert_index, gate_weights, w_gate, w_up, w_down, v_gate, v_up, curvature
):
    experts = lax.axis_size("expert")
    mine = lax.axis_index("expert")
    chosen = expert_index[:, :, None] == jnp.arange(experts, dtype=jnp.int32)[None, None, :]
    gates = jnp.sum(jnp.where(chosen, gate_weights[:, :, None].astype(F32), 0.0), axis=1).astype(BF)
    pad = -experts % 128
    x, all_gates = gather(nz, nx, 0, tokens, jnp.pad(gates, ((0, 0), (0, pad))))
    column = jnp.arange(experts + pad, dtype=jnp.int32)[None, :] == mine
    g = jnp.sum(jnp.where(column, all_gates.astype(F32), 0.0), axis=1, keepdims=True)
    wg, wu, wd, vg, vu = w_gate[0], w_up[0], w_down[0], v_gate[0], v_up[0]
    gate_pre, up_pre, gate_tan, up_tan = dot(x, wg), dot(x, wu), dot(x, vg), dot(x, vu)
    s = jax.nn.sigmoid(gate_pre)
    silu = gate_pre * s
    slope = s * (1.0 + gate_pre * (1.0 - s))
    hidden = (slope * up_pre * gate_tan + silu * up_tan).astype(BF)
    token_tan = scatter(nz, nx, 1, (g * dot(hidden, wd)).astype(BF))
    curved = dot(token_tan, curvature).astype(BF)
    (c,) = gather(nz, nx, 2, curved)
    back = g * dot(c, wd, 1, 1)
    gate_bar = (back * up_pre * slope).astype(BF)
    up_bar = (back * silu).astype(BF)
    gate_term = dot(gate_bar, x, 0, 0).astype(BF)
    up_term = dot(up_bar, x, 0, 0).astype(BF)
    hvp_gate = lax.psum_scatter(gate_term[None], "dp", scatter_dimension=1, tiled=True).astype(F32)
    hvp_up = lax.psum_scatter(up_term[None], "dp", scatter_dimension=1, tiled=True).astype(F32)
    route_in = (dot(gate_bar, wg, 1, 1) + dot(up_bar, wu, 1, 1)).astype(BF)
    return hvp_gate, hvp_up, scatter(nz, nx, 3, route_in)


def solution(mesh):
    experts = mesh.shape["expert"]
    column = mesh.devices.reshape(experts, -1)[:, 0]
    nx = len({device.coords[0] for device in column})
    nx = nx if experts % nx == 0 else 1
    return jax.shard_map(
        functools.partial(shards, experts // nx, nx),
        mesh=mesh,
        in_specs=(
            P(("expert", "dp"), None),
            P(("expert", "dp"), None),
            P(("expert", "dp"), None),
            P("expert", None, None),
            P("expert", None, None),
            P("expert", None, None),
            P("expert", None, None),
            P("expert", None, None),
            P(),
        ),
        out_specs=(P("expert", "dp", None), P("expert", "dp", None), P(("expert", "dp"), None)),
        check_vma=False,
    )
```

time: 408 us -> 301 us (0.74)
  blocking collectives: 223 us -> 0 us
  Pallas kernels: 0 us -> 193 us
  waiting for transfers between devices: 71.7 us -> 8.17 us
  starting transfers between devices: 12 us -> 0.3 us
  matrix products: 75.5 us -> 68.3 us
  local copies, waits for them, and re-layouts: 3.35 us -> 9.82 us
    all_to_all x3 -> x0, blocking collectives: 223 us -> none  [the longest x1 74.5 us: shards(): lax.all_to_all(routed_out.reshape(expert_total, capacity, model_width), '...]
    pallas_call x0 -> x4, Pallas kernels: none -> 193 us  [the longest x2 101 us: gather(): pl.pallas_call(functools.partial(gather_kernel, nz, nx, m), out_shape=[ja...]
    all_to_all x2 -> x0, waiting for transfers between devices: 71.7 us -> none  [the longest x1 69.2 us: shards(): lax.all_to_all(sent_rows.reshape(expert_total, capacity, model_width), 'e...]
    all_to_all x2 -> x0, starting transfers between devices: 11.7 us -> none  [the longest x1 7.25 us: shards(): lax.all_to_all(slot_gates.reshape(expert_total, capacity), 'expert', spli...]
    reduce_scatter x2, waiting for transfers between devices: 0.01 us -> 8.14 us  [the longest x1 8.14 us: shards(): lax.psum_scatter(gate_term[None], 'dp', scatter_dimension=1, tiled=True)]
    dot_general x13 -> x10, matrix products: 75.5 us -> 68.3 us  [dot(): lax.dot_general(a, b, (((ca,), (cb,)), ((), ())), preferred_element_type=...]
    unnamed x17 -> x29, local copies, waits for them, and re-layouts: 1.99 us -> 9.07 us
  transfers between devices with their start and end apart: 4 -> 2, of which waited for: 2 -> 1; matrix products, arithmetic and copies ran while one was open for 7% -> 6% of each run, Pallas kernels for 0% -> 15%
where the time goes in v1:
time: 301 us
  Pallas kernels  193 us (64%)
  matrix products  68.3 us (23%)
  between operations  14.2 us (5%)
  local copies, waits for them, and re-layouts  9.82 us (3%)
  waiting for transfers between devices  8.17 us (3%)
  other arithmetic  6.63 us (2%)
    pallas_call x2, Pallas kernels, gather(): pl.pallas_call(functools.partial(gather_kernel, nz, nx, m), out_shape=[ja...  101 us
    pallas_call x2, Pallas kernels, scatter(): pl.pallas_call(functools.partial(scatter_kernel, nz, nx), out_shape=jax.S...  92.5 us
    dot_general x10, matrix products, dot(): lax.dot_general(a, b, (((ca,), (cb,)), ((), ())), preferred_element_type=...  68.3 us
    unnamed x29, local copies, waits for them, and re-layouts  9.07 us
    reduce_scatter x1, waiting for transfers between devices, shards(): lax.psum_scatter(gate_term[None], 'dp', scatter_dimension=1, tiled=True)  8.14 us
  transfers between devices with their start and end apart: 2, of which 1 were waited for; matrix products, arithmetic and copies ran while one was open for 6% of the time, Pallas kernels for 15%

profile of v1, /device:TPU:0, one launch (start us, length us, event | category | flops | bytes accessed | tf_op | source)
XLA Modules:
  0.0 300.7 jit_solution(13338271807827031049)
XLA Ops:
  7.2 0.0 reduce-scatter.5.cloned.1.call-start
  7.2 0.8 convert_element_type.43
  8.1 0.7 select_reduce_fusion.1
  8.8 0.1 copy.15
  8.9 0.6 pad.4.refs_1_
  9.6 54.5 %shard_map.112 = (bf16[8,128,2048]{2,1,0:T(8,128)(2,1)}, bf16[8,128,128]{2,1,0:T(8,128)(2,1)}) custom-call(bf16[128,2048]{1,0:T(8,128)(2,1)} %refs_0_.1, bf16[128,128]{1,0:T(8,128)(2,1)} %pad.4.refs_1_), custom_call_target="tpu_custom_call" | custom-call | tf_op jit(solution)/shard_map/pallas_call | solution.py:228
  64.1 8.4 %fusion.8 = f32[1024,768]{1,0:T(8,128)} fusion(bf16[1024,2048]{1,0:T(8,128)(2,1)} %bitcast.54, bf16[1,2048,768]{2,1,0:T(8,128)(2,1)} %param.13), kind=kOutput, calls=%fused_computation.12 | convolution fusion | flops 3221225472 | bytes 10485760 | tf_op jit(solution)/shard_map/dot_general | solution.py:16
  72.6 5.2 %fusion.12 = f32[1024,768]{1,0:T(8,128)} fusion(bf16[1024,2048]{1,0:T(8,128)(2,1)S(1)} %bitcast.57, bf16[1,2048,768]{2,1,0:T(8,128)(2,1)S(1)} %copy-done.8), kind=kOutput, calls=%fused_computation.16 | convolution fusion | flops 3221225472 | bytes 10485760 | tf_op jit(solution)/shard_map/dot_general | solution.py:16
  77.7 5.0 %fusion.3 = f32[1024,768]{1,0:T(8,128)} fusion(bf16[1024,2048]{1,0:T(8,128)(2,1)S(1)} %bitcast.58, bf16[1,2048,768]{2,1,0:T(8,128)(2,1)S(1)} %copy-done.7), kind=kOutput, calls=%fused_computation.7 | convolution fusion | flops 3221225472 | bytes 10485760 | tf_op jit(solution)/shard_map/dot_general | solution.py:16
  82.8 0.1 select_reduce_fusion
  82.9 13.9 %multiply_convert_fusion = bf16[1024,2048]{1,0:T(8,128)(2,1)} fusion(f32[1024]{0:T(1024)S(1)} %bitcast.52, bf16[1,768,2048]{2,1,0:T(8,128)(2,1)S(1)} %copy-done, f32[1024,768]{1,0:T(8,128)} %fusion.3, f32[1024,768]{1,0:T(8,128)} %fusion.8, bf16[1024,2048]{1,0:T(8,128)(2,1)} %bitcast.55, bf16[1,2048,768]{2,1,0:T(8,128)(2,1)} %param.15, f32[1024,768]{1,0:T(8,128)} %fusion.12), kind=kOutput, calls=%fused_computation.1 | convolution fusion | flops 6456868864 | bytes 24121344 | tf_op jit(solution)/shard_map/dot_general | solution.py:16
  96.8 2.2 copy-done.2
  99.0 46.2 %shard_map.113 = bf16[128,2048]{1,0:T(8,128)(2,1)S(1)} custom-call(bf16[8,128,2048]{2,1,0:T(8,128)(2,1)S(1)} %bitcast.50), custom_call_target="tpu_custom_call" | custom-call | tf_op jit(solution)/shard_map/pallas_call | solution.py:248
  145.2 5.4 %convolution_convert_fusion.2.refs_0_ = bf16[128,2048]{1,0:T(8,128)(2,1)} fusion(bf16[128,2048]{1,0:T(8,128)(2,1)S(1)} %shard_map.113, bf16[2048,2048]{1,0:T(8,128)(2,1)} %param.17), kind=kOutput, calls=%fused_computation.26 | convolution fusion | flops 1074003968 | bytes 9437184 | tf_op jit(solution)/shard_map/dot_general | solution.py:16
  150.7 46.3 %shard_map.114 = bf16[8,128,2048]{2,1,0:T(8,128)(2,1)} custom-call(bf16[128,2048]{1,0:T(8,128)(2,1)} %convolution_convert_fusion.2.refs_0_), custom_call_target="tpu_custom_call" | custom-call | tf_op jit(solution)/shard_map/pallas_call | solution.py:228
  197.0 9.6 %multiply_convert_fusion.1 = (bf16[1024,768]{1,0:T(8,128)(2,1)S(1)}, bf16[1024,768]{1,0:T(8,128)(2,1)}) fusion(f32[1024]{0:T(1024)S(1)} %bitcast.53, f32[1024,768]{1,0:T(8,128)} %fusion.12, f32[1024,768]{1,0:T(8,128)} %fusion.8, bf16[1024,2048]{1,0:T(8,128)(2,1)} %bitcast.51, bf16[1,768,2048]{2,1,0:T(8,128)(2,1)S(1)} %copy-done), kind=kOutput, calls=%fused_computation.18 | convolution fusion | flops 3232235520 | bytes 16781312 | tf_op jit(solution)/shard_map/dot_general | solution.py:16
  206.6 1.1 copy-done.11
  207.7 4.9 %fusion.16 = bf16[1,768,2048]{2,1,0:T(8,128)(2,1)} fusion(bf16[1024,768]{1,0:T(8,128)(2,1)S(1)} %get-tuple-element.7, bf16[1024,2048]{1,0:T(8,128)(2,1)S(1)} %bitcast.59), kind=kOutput, calls=%fused_computation.25 | convolution fusion | flops 3222798336 | bytes 8912896 | tf_op jit(solution)/shard_map/dot_general | solution.py:16
  212.6 0.0 reduce-scatter.5.cloned.1.call-update
  212.6 0.3 reduce-scatter.3.cloned.1.call-start
  212.9 1.1 copy-done.13
  214.0 7.1 %fusion.15 = bf16[1,768,2048]{2,1,0:T(8,128)(2,1)} fusion(bf16[1024,768]{1,0:T(8,128)(2,1)S(1)} %copy-done.13, bf16[1024,2048]{1,0:T(8,128)(2,1)} %bitcast.56), kind=kOutput, calls=%fused_computation.24 | convolution fusion | flops 3222798336 | bytes 8912896 | tf_op jit(solution)/shard_map/dot_general | solution.py:16
  221.1 0.0 reduce-scatter.3.cloned.1.call-update
  221.1 1.9 copy-done.9
  223.0 5.0 %fusion.10 = f32[1024,2048]{1,0:T(8,128)S(1)} fusion(bf16[1024,768]{1,0:T(8,128)(2,1)} %get-tuple-element.8, bf16[1,2048,768]{2,1,0:T(8,128)(2,1)S(1)} %copy-done.9), kind=kOutput, calls=%fused_computation.14 | convolution fusion | flops 3221225472 | bytes 13107200 | tf_op jit(solution)/shard_map/dot_general | solution.py:16
  228.0 3.8 %add_convert_fusion = bf16[1024,2048]{1,0:T(8,128)(2,1)S(1)} fusion(f32[1024,2048]{1,0:T(8,128)S(1)} %fusion.10, bf16[1024,768]{1,0:T(8,128)(2,1)S(1)} %copy-done.12, bf16[1,2048,768]{2,1,0:T(8,128)(2,1)S(1)} %copy-done.10), kind=kOutput, calls=%fused_computation | convolution fusion | flops 3225419776 | bytes 17301504 | tf_op jit(solution)/shard_map/dot_general | solution.py:16
  231.8 46.3 %shard_map.115 = bf16[128,2048]{1,0:T(8,128)(2,1)S(1)} custom-call(bf16[8,128,2048]{2,1,0:T(8,128)(2,1)S(1)} %bitcast.49), custom_call_target="tpu_custom_call" | custom-call | tf_op jit(solution)/shard_map/pallas_call | solution.py:248
  278.1 0.8 copy-done.3
  278.9 2.5 convert_element_type.54
  281.4 8.1 %reduce-scatter.3.cloned.1.call-done = bf16[1,192,2048]{2,1,0:T(8,128)(2,1)} async-done(((bf16[1,768,2048]{2,1,0:T(8,128)(2,1)}), bf16[1,192,2048]{2,1,0:T(8,128)(2,1)}) %reduce-scatter.3.cloned.1.call-update) | async-done | bytes 786448 | tf_op jit(solution)/shard_map/reduce_scatter | solution.py:295
  289.5 2.5 convert_element_type.51
  292.0 1.9 copy.17
  (25 shorter events, 0.1 us)
Async XLA Ops:
  7.2 75.8 %copy-start = (bf16[1,768,2048]{2,1,0:T(8,128)(2,1)S(1)}, bf16[1,768,2048]{2,1,0:T(8,128)(2,1)}, u32[]{:S(2)}) copy-start(bf16[1,768,2048]{2,1,0:T(8,128)(2,1)} %param.14) | copy-start | bytes 9437188
  7.2 271.7 %reduce-scatter.5.cloned.1.call-start = ((), (), s32[]{:S(2)}) async-start(), calls=%async_computation.3 | async-start | bytes 3932160 | tf_op jit(solution)/shard_map/reduce_scatter | solution.py:296
  64.1 8.5 %copy-start.5 = (bf16[8,128,2048]{2,1,0:T(8,128)(2,1)S(1)}, bf16[8,128,2048]{2,1,0:T(8,128)(2,1)}, u32[]{:S(2)}) copy-start(bf16[8,128,2048]{2,1,0:T(8,128)(2,1)} %get-tuple-element.6) | copy-start | bytes 12582916
  64.1 8.5 %copy-start.8 = (bf16[1,2048,768]{2,1,0:T(8,128)(2,1)S(1)}, bf16[1,2048,768]{2,1,0:T(8,128)(2,1)}, u32[]{:S(2)}) copy-start(bf16[1,2048,768]{2,1,0:T(8,128)(2,1)} %param.12) | copy-start | bytes 9437188
  72.6 5.2 %copy-start.7 = (bf16[1,2048,768]{2,1,0:T(8,128)(2,1)S(1)}, bf16[1,2048,768]{2,1,0:T(8,128)(2,1)}, u32[]{:S(2)}) copy-start(bf16[1,2048,768]{2,1,0:T(8,128)(2,1)} %param.16) | copy-start | bytes 9437188
  77.7 5.1 %copy-start.4 = (bf16[8,128,128]{2,1,0:T(8,128)(2,1)S(1)}, bf16[8,128,128]{2,1,0:T(8,128)(2,1)}, u32[]{:S(2)}) copy-start(bf16[8,128,128]{2,1,0:T(8,128)(2,1)} %get-tuple-element.5) | copy-start | bytes 786436
  96.8 2.2 copy-start.2
  197.0 10.7 %copy-start.6 = (bf16[8,128,2048]{2,1,0:T(8,128)(2,1)S(1)}, bf16[8,128,2048]{2,1,0:T(8,128)(2,1)}, u32[]{:S(2)}) copy-start(bf16[8,128,2048]{2,1,0:T(8,128)(2,1)} %get-tuple-element.6) | copy-start | bytes 12582916
  206.6 1.1 copy-start.11
  212.6 1.4 copy-start.13
  212.6 76.9 %reduce-scatter.3.cloned.1.call-start = ((), (), s32[]{:S(2)}) async-start(), calls=%async_computation.2 | async-start | bytes 3932160 | tf_op jit(solution)/shard_map/reduce_scatter | solution.py:295
  221.1 1.9 copy-start.9
  223.0 5.0 %copy-start.10 = (bf16[1,2048,768]{2,1,0:T(8,128)(2,1)S(1)}, bf16[1,2048,768]{2,1,0:T(8,128)(2,1)}, u32[]{:S(2)}) copy-start(bf16[1,2048,768]{2,1,0:T(8,128)(2,1)} %param.13) | copy-start | bytes 9437188
  223.0 5.0 %copy-start.12 = (bf16[1024,768]{1,0:T(8,128)(2,1)S(1)}, bf16[1024,768]{1,0:T(8,128)(2,1)}, u32[]{:S(2)}) copy-start(bf16[1024,768]{1,0:T(8,128)(2,1)} %copy-done.11) | copy-start | bytes 4718596
  231.8 62.1 %copy-start.1 = (bf16[1,768,2048]{2,1,0:T(8,128)(2,1)S(1)}, bf16[1,768,2048]{2,1,0:T(8,128)(2,1)}, u32[]{:S(2)}) copy-start(bf16[1,768,2048]{2,1,0:T(8,128)(2,1)} %param.14) | copy-start | bytes 9437188
  278.1 0.8 copy-start.3
Sparse Core Ops, SparseCore 0:
  212.7 36.0 reduce-scatter.4
  251.5 37.9 reduce-scatter.2

commit v2 on v1

--- a/solution.py
+++ b/solution.py
@@ -274,10 +274,11 @@
     mine = lax.axis_index("expert")
     chosen = expert_index[:, :, None] == jnp.arange(experts, dtype=jnp.int32)[None, None, :]
     gates = jnp.sum(jnp.where(chosen, gate_weights[:, :, None].astype(F32), 0.0), axis=1).astype(BF)
-    pad = -experts % 128
-    x, all_gates = gather(nz, nx, 0, tokens, jnp.pad(gates, ((0, 0), (0, pad))))
-    column = jnp.arange(experts + pad, dtype=jnp.int32)[None, :] == mine
-    g = jnp.sum(jnp.where(column, all_gates.astype(F32), 0.0), axis=1, keepdims=True)
+    gates = jnp.pad(gates.T, ((0, -experts % 16), (0, 0)))
+    all_gates, x = gather(nz, nx, 0, gates, tokens)
+    all_gates = all_gates.reshape(experts, *gates.shape).astype(F32)
+    is_mine = jnp.arange(gates.shape[0], dtype=jnp.int32)[None, :, None] == mine
+    g = jnp.sum(jnp.where(is_mine, all_gates, 0.0), axis=1).reshape(-1, 1)
     wg, wu, wd, vg, vu = w_gate[0], w_up[0], w_down[0], v_gate[0], v_up[0]
     gate_pre, up_pre, gate_tan, up_tan = dot(x, wg), dot(x, wu), dot(x, vg), dot(x, vu)
     s = jax.nn.sigmoid(gate_pre)

time: 301 us -> 301 us (level)
  transfers between devices with their start and end apart: 2 -> 2, of which waited for: 1 -> 1; matrix products, arithmetic and copies ran while one was open for 6% -> 6% of each run, Pallas kernels for 15% -> 16%
where the time goes in v2:
time: 301 us
  Pallas kernels  191 us (63%)
  matrix products  68.3 us (23%)
  between operations  14.2 us (5%)
  local copies, waits for them, and re-layouts  10.2 us (3%)
  waiting for transfers between devices  9.87 us (3%)
  other arithmetic  6.57 us (2%)
    pallas_call x2, Pallas kernels, gather(): pl.pallas_call(functools.partial(gather_kernel, nz, nx, m), out_shape=[ja...  98.2 us
    pallas_call x2, Pallas kernels, scatter(): pl.pallas_call(functools.partial(scatter_kernel, nz, nx), out_shape=jax.S...  92.9 us
    dot_general x10, matrix products, dot(): lax.dot_general(a, b, (((ca,), (cb,)), ((), ())), preferred_element_type=...  68.3 us
    reduce_scatter x1, waiting for transfers between devices, shards(): lax.psum_scatter(gate_term[None], 'dp', scatter_dimension=1, tiled=True)  9.83 us
    unnamed x29, local copies, waits for them, and re-layouts  9.6 us
  transfers between devices with their start and end apart: 2, of which 1 were waited for; matrix products, arithmetic and copies ran while one was open for 6% of the time, Pallas kernels for 16%

profile of v2, /device:TPU:0, one launch (start us, length us, event | category | flops | bytes accessed | tf_op | source)
XLA Modules:
  0.0 300.6 jit_solution(467746290748133439)
XLA Ops:
  7.2 0.0 copy-start
  7.2 0.0 reduce-scatter.5.cloned.1.call-start
  7.2 0.8 convert_element_type.46
  8.1 0.7 select_reduce_fusion.1
  8.8 0.6 pad.4.refs_0_
  9.4 53.6 %shard_map.112 = (bf16[8,16,128]{2,1,0:T(8,128)(2,1)}, bf16[8,128,2048]{2,1,0:T(8,128)(2,1)}) custom-call(bf16[16,128]{1,0:T(8,128)(2,1)} %pad.4.refs_0_, bf16[128,2048]{1,0:T(8,128)(2,1)} %refs_1_.1), custom_call_target="tpu_custom_call" | custom-call | tf_op jit(solution)/shard_map/pallas_call | solution.py:228
  63.0 8.4 %fusion.8 = f32[1024,768]{1,0:T(8,128)} fusion(bf16[1024,2048]{1,0:T(8,128)(2,1)} %bitcast.58, bf16[1,2048,768]{2,1,0:T(8,128)(2,1)} %param.13), kind=kOutput, calls=%fused_computation.12 | convolution fusion | flops 3221225472 | bytes 10485760 | tf_op jit(solution)/shard_map/dot_general | solution.py:16
  71.5 5.1 %fusion.12 = f32[1024,768]{1,0:T(8,128)} fusion(bf16[1024,2048]{1,0:T(8,128)(2,1)S(1)} %bitcast.61, bf16[1,2048,768]{2,1,0:T(8,128)(2,1)S(1)} %copy-done.8), kind=kOutput, calls=%fused_computation.16 | convolution fusion | flops 3221225472 | bytes 10485760 | tf_op jit(solution)/shard_map/dot_general | solution.py:16
  76.6 5.0 %fusion.3 = f32[1024,768]{1,0:T(8,128)} fusion(bf16[1024,2048]{1,0:T(8,128)(2,1)S(1)} %bitcast.62, bf16[1,2048,768]{2,1,0:T(8,128)(2,1)S(1)} %copy-done.7), kind=kOutput, calls=%fused_computation.7 | convolution fusion | flops 3221225472 | bytes 10485760 | tf_op jit(solution)/shard_map/dot_general | solution.py:16
  81.7 0.1 select_reduce_fusion
  81.8 13.9 %multiply_convert_fusion = bf16[1024,2048]{1,0:T(8,128)(2,1)} fusion(f32[1024]{0:T(1024)S(1)} %bitcast.56, bf16[1,768,2048]{2,1,0:T(8,128)(2,1)S(1)} %copy-done, f32[1024,768]{1,0:T(8,128)} %fusion.3, f32[1024,768]{1,0:T(8,128)} %fusion.8, bf16[1024,2048]{1,0:T(8,128)(2,1)} %bitcast.59, bf16[1,2048,768]{2,1,0:T(8,128)(2,1)} %param.15, f32[1024,768]{1,0:T(8,128)} %fusion.12), kind=kOutput, calls=%fused_computation.1 | convolution fusion | flops 6456868864 | bytes 24121344 | tf_op jit(solution)/shard_map/dot_general | solution.py:16
  95.7 2.2 copy-done.2
  97.9 45.9 %shard_map.113 = bf16[128,2048]{1,0:T(8,128)(2,1)S(1)} custom-call(bf16[8,128,2048]{2,1,0:T(8,128)(2,1)S(1)} %bitcast.53), custom_call_target="tpu_custom_call" | custom-call | tf_op jit(solution)/shard_map/pallas_call | solution.py:248
  143.8 5.4 %convolution_convert_fusion.2.refs_0_ = bf16[128,2048]{1,0:T(8,128)(2,1)} fusion(bf16[128,2048]{1,0:T(8,128)(2,1)S(1)} %shard_map.113, bf16[2048,2048]{1,0:T(8,128)(2,1)} %param.17), kind=kOutput, calls=%fused_computation.26 | convolution fusion | flops 1074003968 | bytes 9437184 | tf_op jit(solution)/shard_map/dot_general | solution.py:16
  149.2 44.6 %shard_map.114 = bf16[8,128,2048]{2,1,0:T(8,128)(2,1)} custom-call(bf16[128,2048]{1,0:T(8,128)(2,1)} %convolution_convert_fusion.2.refs_0_), custom_call_target="tpu_custom_call" | custom-call | tf_op jit(solution)/shard_map/pallas_call | solution.py:228
  193.9 9.6 %multiply_convert_fusion.1 = (bf16[1024,768]{1,0:T(8,128)(2,1)S(1)}, bf16[1024,768]{1,0:T(8,128)(2,1)}) fusion(f32[1024]{0:T(1024)S(1)} %bitcast.57, f32[1024,768]{1,0:T(8,128)} %fusion.12, f32[1024,768]{1,0:T(8,128)} %fusion.8, bf16[1024,2048]{1,0:T(8,128)(2,1)} %bitcast.54, bf16[1,768,2048]{2,1,0:T(8,128)(2,1)S(1)} %copy-done), kind=kOutput, calls=%fused_computation.18 | convolution fusion | flops 3232235520 | bytes 16781312 | tf_op jit(solution)/shard_map/dot_general | solution.py:16
  203.5 1.1 copy-done.11
  204.6 4.9 %fusion.16 = bf16[1,768,2048]{2,1,0:T(8,128)(2,1)} fusion(bf16[1024,768]{1,0:T(8,128)(2,1)S(1)} %get-tuple-element.7, bf16[1024,2048]{1,0:T(8,128)(2,1)S(1)} %bitcast.63), kind=kOutput, calls=%fused_computation.25 | convolution fusion | flops 3222798336 | bytes 8912896 | tf_op jit(solution)/shard_map/dot_general | solution.py:16
  209.5 0.0 reduce-scatter.5.cloned.1.call-update
  209.5 0.3 reduce-scatter.3.cloned.1.call-start
  209.8 1.1 copy-done.13
  210.9 7.0 %fusion.15 = bf16[1,768,2048]{2,1,0:T(8,128)(2,1)} fusion(bf16[1024,768]{1,0:T(8,128)(2,1)S(1)} %copy-done.13, bf16[1024,2048]{1,0:T(8,128)(2,1)} %bitcast.60), kind=kOutput, calls=%fused_computation.24 | convolution fusion | flops 3222798336 | bytes 8912896 | tf_op jit(solution)/shard_map/dot_general | solution.py:16
  217.9 0.0 reduce-scatter.3.cloned.1.call-update
  218.0 2.4 copy-done.9
  220.4 5.1 %fusion.10 = f32[1024,2048]{1,0:T(8,128)S(1)} fusion(bf16[1024,768]{1,0:T(8,128)(2,1)} %get-tuple-element.8, bf16[1,2048,768]{2,1,0:T(8,128)(2,1)S(1)} %copy-done.9), kind=kOutput, calls=%fused_computation.14 | convolution fusion | flops 3221225472 | bytes 13107200 | tf_op jit(solution)/shard_map/dot_general | solution.py:16
  225.5 3.8 %add_convert_fusion = bf16[1024,2048]{1,0:T(8,128)(2,1)S(1)} fusion(f32[1024,2048]{1,0:T(8,128)S(1)} %fusion.10, bf16[1024,768]{1,0:T(8,128)(2,1)S(1)} %copy-done.12, bf16[1,2048,768]{2,1,0:T(8,128)(2,1)S(1)} %copy-done.10), kind=kOutput, calls=%fused_computation | convolution fusion | flops 3225419776 | bytes 17301504 | tf_op jit(solution)/shard_map/dot_general | solution.py:16
  229.3 47.0 %shard_map.115 = bf16[128,2048]{1,0:T(8,128)(2,1)S(1)} custom-call(bf16[8,128,2048]{2,1,0:T(8,128)(2,1)S(1)} %bitcast.52), custom_call_target="tpu_custom_call" | custom-call | tf_op jit(solution)/shard_map/pallas_call | solution.py:248
  276.3 0.8 copy-done.3
  277.1 2.5 convert_element_type.58
  279.5 9.8 %reduce-scatter.3.cloned.1.call-done = bf16[1,192,2048]{2,1,0:T(8,128)(2,1)} async-done(((bf16[1,768,2048]{2,1,0:T(8,128)(2,1)}), bf16[1,192,2048]{2,1,0:T(8,128)(2,1)}) %reduce-scatter.3.cloned.1.call-update) | async-done | bytes 786448 | tf_op jit(solution)/shard_map/reduce_scatter | solution.py:296
  289.4 2.5 convert_element_type.55
  291.8 1.9 copy.15
  (24 shorter events, 0.1 us)
Async XLA Ops:
  7.2 74.6 %copy-start = (bf16[1,768,2048]{2,1,0:T(8,128)(2,1)S(1)}, bf16[1,768,2048]{2,1,0:T(8,128)(2,1)}, u32[]{:S(2)}) copy-start(bf16[1,768,2048]{2,1,0:T(8,128)(2,1)} %param.14) | copy-start | bytes 9437188
  7.2 269.9 %reduce-scatter.5.cloned.1.call-start = ((), (), s32[]{:S(2)}) async-start(), calls=%async_computation.3 | async-start | bytes 3932160 | tf_op jit(solution)/shard_map/reduce_scatter | solution.py:297
  63.0 8.5 %copy-start.5 = (bf16[8,128,2048]{2,1,0:T(8,128)(2,1)S(1)}, bf16[8,128,2048]{2,1,0:T(8,128)(2,1)}, u32[]{:S(2)}) copy-start(bf16[8,128,2048]{2,1,0:T(8,128)(2,1)} %get-tuple-element.6) | copy-start | bytes 12582916
  63.0 8.5 %copy-start.8 = (bf16[1,2048,768]{2,1,0:T(8,128)(2,1)S(1)}, bf16[1,2048,768]{2,1,0:T(8,128)(2,1)}, u32[]{:S(2)}) copy-start(bf16[1,2048,768]{2,1,0:T(8,128)(2,1)} %param.12) | copy-start | bytes 9437188
  71.5 5.2 %copy-start.7 = (bf16[1,2048,768]{2,1,0:T(8,128)(2,1)S(1)}, bf16[1,2048,768]{2,1,0:T(8,128)(2,1)}, u32[]{:S(2)}) copy-start(bf16[1,2048,768]{2,1,0:T(8,128)(2,1)} %param.16) | copy-start | bytes 9437188
  76.6 5.1 %copy-start.4 = (bf16[8,16,128]{2,1,0:T(8,128)(2,1)S(1)}, bf16[8,16,128]{2,1,0:T(8,128)(2,1)}, u32[]{:S(2)}) copy-start(bf16[8,16,128]{2,1,0:T(8,128)(2,1)} %get-tuple-element.5) | copy-start | bytes 98308
  95.7 2.2 copy-start.2
  193.9 10.7 %copy-start.6 = (bf16[8,128,2048]{2,1,0:T(8,128)(2,1)S(1)}, bf16[8,128,2048]{2,1,0:T(8,128)(2,1)}, u32[]{:S(2)}) copy-start(bf16[8,128,2048]{2,1,0:T(8,128)(2,1)} %get-tuple-element.6) | copy-start | bytes 12582916
  203.5 1.1 copy-start.11
  209.5 1.4 copy-start.13
  209.5 79.9 %reduce-scatter.3.cloned.1.call-start = ((), (), s32[]{:S(2)}) async-start(), calls=%async_computation.2 | async-start | bytes 3932160 | tf_op jit(solution)/shard_map/reduce_scatter | solution.py:296
  217.9 2.5 copy-start.9
  220.4 5.1 %copy-start.10 = (bf16[1,2048,768]{2,1,0:T(8,128)(2,1)S(1)}, bf16[1,2048,768]{2,1,0:T(8,128)(2,1)}, u32[]{:S(2)}) copy-start(bf16[1,2048,768]{2,1,0:T(8,128)(2,1)} %param.13) | copy-start | bytes 9437188
  220.4 5.1 %copy-start.12 = (bf16[1024,768]{1,0:T(8,128)(2,1)S(1)}, bf16[1024,768]{1,0:T(8,128)(2,1)}, u32[]{:S(2)}) copy-start(bf16[1024,768]{1,0:T(8,128)(2,1)} %copy-done.11) | copy-start | bytes 4718596
  229.3 64.4 %copy-start.1 = (bf16[1,768,2048]{2,1,0:T(8,128)(2,1)S(1)}, bf16[1,768,2048]{2,1,0:T(8,128)(2,1)}, u32[]{:S(2)}) copy-start(bf16[1,768,2048]{2,1,0:T(8,128)(2,1)} %param.14) | copy-start | bytes 9437188
  276.3 0.8 copy-start.3
Sparse Core Ops, SparseCore 0:
  209.6 39.0 reduce-scatter.4
  251.4 37.9 reduce-scatter.2
